TPU v7x, 256 devices: a whole 4x4x8 slice. The times are simulated.
256 devices in a mesh: seq: 32 (over z, x), head: 8 (over y, core).
Axes of the slice: x: 4, y: 4, z: 8, core: 2. Of those that a mesh axis runs over, the one named last changes fastest.
Arguments:
- queries: bfloat16 [16384, 6144], P('seq', 'head'), may hold values from -0.5 to 0.5
- keys: bfloat16 [16384, 6144], P('seq', 'head'), may hold values from -0.5 to 0.5
- values: bfloat16 [16384, 6144], P('seq', 'head'), may hold values from -6 to 6
- doc_lengths: int32 [32], replicated, may hold values from 1 to 12288, 16384 in all
- decay_rates: float32 [48], P('head'), may hold values from 1.8310548e-05 to 0.06
- gain: float32 [6144], P('head'), may hold values from 0.5 to 1.5
- out_grad: bfloat16 [16384, 6144], P('seq', 'head'), may hold values from -6 to 6
Outputs:
- grad_queries: bfloat16 [16384, 6144], P('seq', 'head')
- grad_keys: bfloat16 [16384, 6144], P('seq', 'head')
- grad_values: bfloat16 [16384, 6144], P('seq', 'head')
- gain_grad: float32 [6144], P('head')
Inputs may be any that keep to these rules, and one draw needn't show every extreme that they name: `doc_lengths`: document lengths in order; they sum to 16384 and the longest is exactly 12288.
All inputs are finite; a program needn't handle non-finite values.
Results may differ from a plain program's by a relative error of at most 0.013.
Values may be sent and summed in bfloat16 or wider, within the bound.
A program may use at most 128 MiB of HBM per device.

v0:
```python
import math

import jax
import jax.numpy as jnp
from jax import lax
from jax.sharding import PartitionSpec as P

EPS = 1e-06


def prefix(value, axis, join, neutral):
    count, mine = (lax.axis_size(axis), lax.axis_index(axis))
    pieces = jax.tree.map(lambda part: lax.all_gather(part, axis), value)
    pieces = jax.tree.map(lambda part: part[::-1], pieces)
    mine = count - 1 - mine
    running = jax.tree.map(
        lambda part, zero: jnp.full_like(part, 0) + jnp.asarray(zero, part.dtype), value, neutral
    )

    def lap(position, running):
        longer = join(running, jax.tree.map(lambda part: part[position], pieces))
        return jax.tree.map(lambda new, old: jnp.where(position < mine, new, old), longer, running)

    return lax.fori_loop(0, count - 1, lap, running)


def doc_index(ends, positions):
    return jnp.sum((ends[None, :] <= positions[:, None]).astype(jnp.int32), axis=1)


def chain_combine(earlier, later):
    return (earlier[0] * later[0], earlier[1] * later[0][:, None, None] + later[1])


def on_device(queries, keys, values, doc_lengths, decay_rates, gain, out_grad):
    count = queries.shape[0]
    heads = decay_rates.shape[0]
    width = queries.shape[1] // heads
    blocks = lax.axis_size("seq")
    here = lax.axis_index("seq")
    total = queries.shape[1] * lax.axis_size("head")
    first_tok = here * count
    ends = jnp.cumsum(doc_lengths)
    offsets = jnp.arange(count, dtype=jnp.int32)
    seg_tok = doc_index(ends, first_tok + offsets)
    rims = doc_index(ends, jnp.stack([first_tok - 1, first_tok + count - 1]))
    prev_seg = rims[0]
    last_seg = rims[1]
    upos = offsets.astype(jnp.float32)
    rates = decay_rates[None, :]
    w_in = (
        jnp.exp(-rates * (upos[:, None] + 1.0)) * (seg_tok == prev_seg).astype(jnp.float32)[:, None]
    )
    w_out = (
        jnp.exp(-rates * (count - 1.0 - upos[:, None]))
        * (seg_tok == last_seg).astype(jnp.float32)[:, None]
    )
    diff = upos[:, None] - upos[None, :]
    keep = (diff >= 0.0) & (seg_tok[:, None] == seg_tok[None, :])
    mask = jnp.where(
        keep[None], jnp.exp(-decay_rates[:, None, None] * jnp.maximum(diff, 0.0)[None]), 0.0
    )
    through = jnp.exp(-decay_rates * count) * (prev_seg == last_seg).astype(jnp.float32)
    query_heads = queries.reshape(count, heads, width)
    key_heads = keys.reshape(count, heads, width)
    value_heads = values.reshape(count, heads, width)
    keys_scaled = (key_heads.astype(jnp.float32) * w_out[:, :, None]).astype(jnp.bfloat16)
    states = jnp.einsum(
        "tha,thb->hab", keys_scaled, value_heads, preferred_element_type=jnp.float32
    ).astype(jnp.bfloat16)
    zeros = jnp.zeros(states.shape, jnp.float32)
    ones = jnp.ones((heads,), jnp.float32)
    piece = lax.all_gather(states[None], "seq", axis=0, tiled=True)
    index = jnp.arange(piece.shape[0], dtype=jnp.int32)
    seg_end = doc_index(ends, (index + 1) * count - 1)
    linked = (index < here) & (seg_end == prev_seg)
    gap = jnp.maximum(here - 1 - index, 0).astype(jnp.float32)
    factor = jnp.where(linked[:, None], jnp.exp(-rates * count * gap[:, None]), 0.0)
    incoming = jnp.einsum(
        "nh,nhab->hab", factor, piece.astype(jnp.float32), precision=lax.Precision.HIGHEST
    )
    incoming = incoming.astype(jnp.bfloat16)
    scores = jnp.einsum("tha,sha->hts", query_heads, key_heads, preferred_element_type=jnp.float32)
    weights = (scores * mask).astype(jnp.bfloat16)
    attended = jnp.einsum("hts,shb->thb", weights, value_heads, preferred_element_type=jnp.float32)
    attended = attended + w_in[:, :, None] * jnp.einsum(
        "tha,hab->thb", query_heads, incoming, preferred_element_type=jnp.float32
    )
    flat = attended.reshape(count, heads * width)
    dyf = out_grad.astype(jnp.float32)
    scaled_grad = gain[None, :] * dyf
    sums = lax.psum((jnp.sum(flat * flat, axis=1), jnp.sum(scaled_grad * flat, axis=1)), "head")
    inv = lax.rsqrt(sums[0] / total + EPS)
    gain_grad = lax.psum(jnp.sum(dyf * flat * inv[:, None], axis=0), "seq") * (
        1.0 / math.sqrt(count * blocks)
    )
    dout = (
        inv[:, None] * scaled_grad - flat * (inv * inv * inv * sums[1] / total)[:, None]
    ).astype(jnp.bfloat16)
    back = dout.reshape(count, heads, width)
    dweights = (
        jnp.einsum("thb,shb->hts", back, value_heads, preferred_element_type=jnp.float32) * mask
    ).astype(jnp.bfloat16)
    queries_scaled = (query_heads.astype(jnp.float32) * w_in[:, :, None]).astype(jnp.bfloat16)
    grads = jnp.einsum(
        "tha,thb->hab", queries_scaled, back, preferred_element_type=jnp.float32
    ).astype(jnp.bfloat16)
    outgoing = prefix((through, grads.astype(jnp.float32)), "seq", chain_combine, (ones, zeros))[1]
    outgoing = outgoing.astype(jnp.bfloat16)
    grad_q = jnp.einsum("hts,sha->tha", dweights, key_heads, preferred_element_type=jnp.float32)
    grad_q = grad_q + w_in[:, :, None] * jnp.einsum(
        "thb,hab->tha", back, incoming, preferred_element_type=jnp.float32
    )
    grad_k = jnp.einsum("hts,tha->sha", dweights, query_heads, preferred_element_type=jnp.float32)
    grad_k = grad_k + w_out[:, :, None] * jnp.einsum(
        "thb,hab->tha", value_heads, outgoing, preferred_element_type=jnp.float32
    )
    grad_v = jnp.einsum("hts,tha->sha", weights, back, preferred_element_type=jnp.float32)
    grad_v = grad_v + w_out[:, :, None] * jnp.einsum(
        "tha,hab->thb", key_heads, outgoing, preferred_element_type=jnp.float32
    )
    shape_out = (count, heads * width)
    return (
        grad_q.reshape(shape_out).astype(jnp.bfloat16),
        grad_k.reshape(shape_out).astype(jnp.bfloat16),
        grad_v.reshape(shape_out).astype(jnp.bfloat16),
        gain_grad,
    )


def solution(mesh):
    return jax.shard_map(
        on_device,
        mesh=mesh,
        in_specs=(
            P("seq", "head"),
            P("seq", "head"),
            P("seq", "head"),
            P(),
            P("head"),
            P("head"),
            P("seq", "head"),
        ),
        out_specs=(P("seq", "head"), P("seq", "head"), P("seq", "head"), P("head")),
        check_vma=False,
    )
```

profile of v0, /device:TPU:2, one launch (start us, length us, event | category | flops | bytes accessed | tf_op | source)
XLA Modules:
  0.0 339.9 jit_solution(2191930614392643774)
XLA Ops:
  7.3 0.8 copy.78
  10.5 1.3 compare_convert_fusion
  11.8 1.4 copy.75
  15.0 1.0 convolution_convert_fusion.1
  17.5 1.7 copy.74
  19.7 1.9 multiply_convert_fusion.1
  21.6 1.6 copy-done
  23.3 2.3 fusion.31
  25.5 81.1 %all-gather.6.cloned.1.call-done = bf16[192,128,128]{2,1,0:T(8,128)(2,1)} async-done(((bf16[6,128,128]{2,1,0:T(8,128)(2,1)}), bf16[192,128,128]{2,1,0:T(8,128)(2,1)}) %all-gather.6.cloned.1.call-update) | async-done | bytes 6291472 | tf_op jit(solution)/shard_map/all_gather | solution.py:73
  106.7 9.0 %fusion.1 = f32[6,1,128,128]{3,1,2,0:T(1,128)S(1)} fusion(f32[32,6,1,1]{0,2,3,1:T(1,128)S(1)} %copy.97, bf16[32,6,128,128]{3,2,1,0:T(8,128)(2,1)} %bitcast.84), kind=kOutput, calls=%fused_computation.3 | convolution fusion | flops 37748736 | bytes 6685440 | tf_op jit(solution)/shard_map/nh,nhab->hab/dot_general | solution.py:79
  116.4 14.2 %psum.21 = f32[512]{0:T(512)S(1)} all-reduce(f32[512]{0:T(512)S(1)} %get-tuple-element.156), channel_id=1, replica_groups=mesh['seq'=32,'head'=8] {'head'}, use_global_device_ids=true, to_apply=%region_5.6 | all-reduce | flops 512 | bytes 4096 | tf_op jit(solution)/shard_map/psum | solution.py:92
  131.2 12.4 %psum.22 = f32[512]{0:T(512)S(1)} all-reduce(f32[512]{0:T(512)S(1)} %get-tuple-element.134), channel_id=1, replica_groups=mesh['seq'=32,'head'=8] {'head'}, use_global_device_ids=true, to_apply=%region_7.8 | all-reduce | flops 512 | bytes 4096 | tf_op jit(solution)/shard_map/psum | solution.py:92
  143.7 1.5 fusion.6
  145.2 1.1 fusion.17
  146.4 74.3 %all-reduce.1 = (f32[192]{0:T(256)S(1)}, f32[768]{0:T(1024)}) all-reduce(f32[192]{0:T(256)S(1)} %get-tuple-element.149, f32[768]{0:T(1024)S(1)} %get-tuple-element.133), channel_id=3, replica_groups=mesh['seq'=32,'head'=8] {'seq'}, use_global_device_ids=true, to_apply=%add | all-reduce | flops 960 | bytes 7680
  221.3 3.2 multiply_convert_fusion
  224.6 1.1 fusion.32
  226.3 2.6 fusion.15
  228.8 2.3 copy.91
  231.7 3.1 fusion.33
  235.4 25.4 %all-gather.8.cloned.1.call-done = f32[192,128,128]{2,1,0:T(8,128)} async-done(((f32[6,128,128]{2,1,0:T(8,128)}), f32[192,128,128]{2,1,0:T(8,128)}) %all-gather.8.cloned.1.call-update) | async-done | bytes 12582928 | tf_op jit(solution)/shard_map/all_gather | solution.py:13
  260.9 11.2 %rev.7 = f32[32,6,128,128]{3,2,1,0:T(8,128)} reverse(f32[32,6,128,128]{3,2,1,0:T(8,128)} %bitcast.85), dimensions={0} | reverse | bytes 25165824 | tf_op jit(solution)/shard_map/rev | solution.py:14
  272.1 56.5 %while.14 = (s32[]{:T(128)}, f32[6,128,128]{2,1,0:T(8,128)S(1)}, s32[]{:T(128)}, f32[32,6]{1,0:T(8,128)}, f32[32,6,128,128]{3,2,1,0:T(8,128)}, /*index=5*/s32[]{:T(128)}, s32[]{:T(128)}) while((s32[]{:T(128)}, f32[6,128,128]{2,1,0:T(8,128)S(1)}, s32[]{:T(128)}, f32[32,6]{1,0:T(8,128)}, f32[32,6,128,128]{3,2,1,0:T(8,128)}, ...), condition=%wide.region_9.10_spmd.clone, body=%wide.region_8.9_spmd.clone.sunk | while | flops 393220 | bytes 1179833 | solution.py:24
  272.1 0.8 dynamic-slice_bitcast_fusion.2
  272.9 1.1 fusion.55
  274.7 1.1 fusion.55
  276.5 1.1 fusion.55
  278.3 1.1 fusion.55
  280.1 1.1 fusion.55
  281.9 1.1 fusion.55
  283.8 1.1 fusion.55
  285.6 1.1 fusion.55
  286.7 0.7 dynamic-slice_bitcast_fusion.2
  287.4 1.1 fusion.55
  288.5 0.7 dynamic-slice_bitcast_fusion.2
  289.2 1.1 fusion.55
  290.4 0.7 dynamic-slice_bitcast_fusion.2
  291.1 1.1 fusion.55
  292.2 0.7 dynamic-slice_bitcast_fusion.2
  292.9 1.1 fusion.55
  294.7 1.1 fusion.55
  295.8 0.7 dynamic-slice_bitcast_fusion.2
  296.5 1.1 fusion.55
  297.7 0.7 dynamic-slice_bitcast_fusion.2
  298.3 1.1 fusion.55
  300.2 1.1 fusion.55
  302.0 1.1 fusion.55
  303.8 1.1 fusion.55
  305.6 1.1 fusion.55
  307.4 1.1 fusion.55
  309.3 1.1 fusion.55
  311.1 1.1 fusion.55
  312.9 1.1 fusion.55
  314.7 1.1 fusion.55
  316.5 1.1 fusion.55
  318.3 1.1 fusion.55
  320.2 1.1 fusion.55
  322.0 1.1 fusion.55
  323.8 1.1 fusion.55
  325.6 1.1 fusion.55
  327.4 1.1 fusion.55
  328.6 1.8 fusion.11
  330.4 1.2 copy.93
  331.9 1.2 copy.92
  (112 shorter events, 24.6 us)
Async XLA Ops:
  7.2 6.1 %copy-start.18 = (bf16[512,768]{1,0:T(8,128)(2,1)S(1)}, bf16[512,768]{1,0:T(8,128)(2,1)}, u32[]{:S(2)}) copy-start(bf16[512,768]{1,0:T(8,128)(2,1)} %param.11) | copy-start | bytes 2359300
  7.2 99.5 %all-gather.6.cloned.1.call-start = ((), (), s32[]{:S(2)}) async-start(), calls=%async_computation | async-start | bytes 6488064 | tf_op jit(solution)/shard_map/all_gather | solution.py:73
  11.8 1.8 copy-start.25
  11.8 3.0 copy-start.24
  13.2 6.5 %copy-start.10 = (bf16[512,768]{0,1:T(8,128)(2,1)}, bf16[512,768]{0,1:T(8,128)(2,1)S(1)}, u32[]{:S(2)}) copy-start(bf16[512,768]{0,1:T(8,128)(2,1)S(1)} %copy.75) | copy-start | bytes 2359300
  13.2 3.9 %copy-start.19 = (bf16[512,768]{1,0:T(8,128)(2,1)S(1)}, bf16[512,768]{1,0:T(8,128)(2,1)}, u32[]{:S(2)}) copy-start(bf16[512,768]{1,0:T(8,128)(2,1)} %param.15) | copy-start | bytes 2359300
  13.5 8.1 %copy-start.7 = (bf16[512,768]{0,1:T(8,128)(2,1)}, bf16[512,768]{0,1:T(8,128)(2,1)S(1)}, u32[]{:S(2)}) copy-start(bf16[512,768]{0,1:T(8,128)(2,1)S(1)} %copy.79) | copy-start | bytes 2359300
  15.0 2.5 copy-start.20
  16.1 244.8 %all-gather.8.cloned.1.call-start = ((), (), s32[]{:S(2)}) async-start(), calls=%async_computation.1 | async-start | bytes 12976128 | tf_op jit(solution)/shard_map/all_gather | solution.py:13
  17.5 113.2 %copy-start.13 = (bf16[512,768]{0,1:T(8,128)(2,1)}, bf16[512,768]{0,1:T(8,128)(2,1)S(1)}, u32[]{:S(2)}) copy-start(bf16[512,768]{0,1:T(8,128)(2,1)S(1)} %copy.83) | copy-start | bytes 2359300
  19.2 126.0 %copy-start.5 = (bf16[512,768]{0,1:T(8,128)(2,1)}, bf16[512,768]{0,1:T(8,128)(2,1)S(1)}, u32[]{:S(2)}) copy-start(bf16[512,768]{0,1:T(8,128)(2,1)S(1)} %copy.74) | copy-start | bytes 2359300
  19.7 1.9 copy-start.17
  21.6 1.6 copy-start
  106.7 9.0 %copy-start.14 = (f32[6,512,128]{1,2,0:T(8,128)S(1)}, f32[6,512,128]{1,2,0:T(8,128)}, u32[]{:S(2)}) copy-start(f32[6,512,128]{1,2,0:T(8,128)} %fusion.31) | copy-start | bytes 4718596
  115.7 0.7 copy-start.15
  115.7 14.9 %copy-start.22 = (f32[768]{0:T(1024)S(1)}, f32[768]{0:T(1024)}, u32[]{:S(2)}) copy-start(f32[768]{0:T(1024)} %param.14) | copy-start | bytes 9220
  145.2 79.4 %copy-start.4 = (bf16[512,768]{0,1:T(8,128)(2,1)}, bf16[512,768]{0,1:T(8,128)(2,1)S(1)}, u32[]{:S(2)}) copy-start(bf16[512,768]{0,1:T(8,128)(2,1)S(1)} %fusion.6) | copy-start | bytes 2359300
  145.2 76.2 %copy-start.8 = (bf16[512,768]{0,1:T(8,128)(2,1)S(1)}, bf16[512,768]{0,1:T(8,128)(2,1)}, u32[]{:S(2)}) copy-start(bf16[512,768]{0,1:T(8,128)(2,1)} %copy-done.7) | copy-start | bytes 2359300
  221.3 3.3 copy-start.11
  224.6 1.7 copy-start.2
  224.6 1.7 copy-start.16
  226.3 5.5 %copy-start.1 = (bf16[6,512,512]{2,1,0:T(8,128)(2,1)S(1)}, bf16[6,512,512]{2,1,0:T(8,128)(2,1)}, u32[]{:S(2)}) copy-start(bf16[6,512,512]{2,1,0:T(8,128)(2,1)} %copy-done) | copy-start | bytes 9437188
  228.8 2.3 copy-start.23
  231.7 3.1 copy-start.3
  231.7 3.1 copy-start.6
  272.1 56.5 %copy-start.12 = (bf16[512,768]{0,1:T(8,128)(2,1)S(1)}, bf16[512,768]{0,1:T(8,128)(2,1)}, u32[]{:S(2)}) copy-start(bf16[512,768]{0,1:T(8,128)(2,1)} %copy-done.10) | copy-start | bytes 2359300
  272.1 56.5 %copy-start.21 = (f32[512,6]{0,1:T(8,128)S(1)}, f32[512,6]{0,1:T(8,128)}, u32[]{:S(2)}) copy-start(f32[512,6]{0,1:T(8,128)} %copy-done.20) | copy-start | bytes 36868
  330.4 1.2 copy-start.9
Sparse Core Ops, SparseCore 0:
  16.2 90.3 all-gather.5
  146.5 114.3 all-gather.7
where the time goes:
time: 344 us; the launch traced here: 340 us
  waiting for transfers between devices  107 us (31%)
  blocking collectives  101 us (29%)
  local copies, waits for them, and re-layouts  46.1 us (13%)
  other arithmetic  40.4 us (12%)
  matrix products  28.7 us (8%)
  between operations  16.5 us (5%)
    all_gather x1, waiting for transfers between devices, on_device(): piece = lax.all_gather(states[None], 'seq', axis=0, tiled=True)  81.1 us
    unnamed x1, blocking collectives  74.3 us
    select_n x31, other arithmetic, lap(): jnp.where(position < mine, new, old)  34.4 us
    psum x2, blocking collectives, on_device(): lax.psum((jnp.sum(flat * flat, axis=1), jnp.sum(scaled_grad * flat, axis=...  26.6 us
    all_gather x1, waiting for transfers between devices, prefix(): pieces = jax.tree.map(lambda part: lax.all_gather(part, axis), value)  25.4 us
    mul x31, local copies, waits for them, and re-layouts, chain_combine(): earlier[1] * later[0][:, None, None] + later[1]  21.3 us
    rev x2, local copies, waits for them, and re-layouts, prefix(): pieces = jax.tree.map(lambda part: part[::-1], pieces)  11.9 us
    unnamed x61, local copies, waits for them, and re-layouts  11.4 us
  transfers between devices with their start and end apart: 2, of which 2 were waited for; matrix products, arithmetic and copies ran while one was open for 6% of the time, Pallas kernels for 0%

commit v1 on v0

v1 whole, which is shorter than its diff:
```python
import math

import jax
import jax.numpy as jnp
from jax import lax
from jax.experimental import pallas as pl
from jax.experimental.pallas import tpu as pltpu
from jax.sharding import PartitionSpec as P

EPS = 1e-06
MESH = pl.DeviceIdType.MESH
F32 = jnp.float32
BF16 = jnp.bfloat16
NT = (((1,), (1,)), ((), ()))
TN = (((0,), (0,)), ((), ()))
NN = (((1,), (0,)), ((), ()))

T = 512
HALF = T // 2
W = 128
H = 6
FEATURES = 6144
TOKENS = 16384
SEQ = 32
M = 8
G = SEQ // M
ROWS = W // M
NHEAD = 8
DOCS = 32


def dot(a, b, dims):
    return lax.dot_general(a, b, dims, preferred_element_type=F32)


def kernel(
    docs,
    rates,
    gain,
    q_hbm,
    k_hbm,
    v_hbm,
    og_hbm,
    gq_hbm,
    gk_hbm,
    gv_hbm,
    gg_ref,
    q_s,
    k_s,
    v_s,
    og_s,
    w_s,
    dw_s,
    keep_s,
    att_s,
    d_s,
    qt_s,
    dk_s,
    dv_s,
    gq_s,
    gk_s,
    gv_s,
    share_out,
    share_in,
    tot_out,
    tot_in,
    carry_s,
    loc_s,
    back_out,
    back_in,
    sum_out,
    sum_in,
    gain_mine,
    gain_in,
    gain_tot,
    gain_all,
    in_sem,
    out_sem,
    share_ss,
    share_rs,
    tot_ss,
    tot_rs,
    back_ss,
    back_rs,
    sum_ss,
    sum_rs,
    ga_ss,
    ga_rs,
    gb_ss,
    gb_rs,
):
    s = lax.axis_index("seq")
    hd = lax.axis_index("head")
    g = s // M
    m = lax.rem(s, M)

    def member(i):
        return (g * M + i, hd)

    def peer(k):
        return lax.rem(m + k, M)

    barrier = pltpu.get_barrier_semaphore()
    for k in range(1, M):
        pl.semaphore_signal(barrier, inc=1, device_id=member(peer(k)), device_id_type=MESH)
    for k in range(1, G):
        pl.semaphore_signal(
            barrier, inc=1, device_id=(lax.rem(s + k * M, SEQ), hd), device_id_type=MESH
        )
    for k in range(1, NHEAD):
        pl.semaphore_signal(
            barrier, inc=1, device_id=(s, lax.rem(hd + k, NHEAD)), device_id_type=MESH
        )

    hbm = (k_hbm, v_hbm, q_hbm, og_hbm)
    vmem = (k_s, v_s, q_s, og_s)

    def load(a, h):
        cols = pl.ds(pl.multiple_of(h * W, W), W)
        return pltpu.make_async_copy(hbm[a].at[:, cols], vmem[a].at[h], in_sem.at[a, h])

    for h in range(H):
        load(0, h).start()
        load(1, h).start()
    for h in range(H):
        load(2, h).start()
    for h in range(H):
        load(3, h).start()

    begin = s * T
    far = jnp.int32(1 << 24)
    total = jnp.int32(0)
    bits = jnp.int32(0)
    first_end = far
    last_start = -far
    rel = []
    for d in range(DOCS):
        total = total + docs[d]
        here = total - begin
        rel.append(here)
        if d < DOCS - 1:
            bits = bits | lax.shift_left(jnp.int32(1), lax.shift_right_logical(total, 9))
        first_end = jnp.where((here >= 0) & (first_end == far), here, first_end)
        last_start = jnp.where(here <= T - 1, here, last_start)

    def clear(at, count):
        if count == 0:
            return jnp.float32(1.0)
        field = lax.shift_right_logical(bits, at) & jnp.int32((1 << count) - 1)
        return jnp.where(field == 0, jnp.float32(1.0), jnp.float32(0.0))

    ucol = lax.broadcasted_iota(jnp.int32, (T, W), 0)
    ucol_f = ucol.astype(F32)
    urow_f = lax.broadcasted_iota(jnp.int32, (1, T), 1).astype(F32)

    def w_in_of(r):
        return jnp.where(ucol < first_end, jnp.exp(-r * (ucol_f + 1.0)), 0.0)

    def w_out_of(r):
        return jnp.where(ucol >= last_start, jnp.exp(-r * (T - 1.0 - ucol_f)), 0.0)

    def power(r, n):
        return jnp.exp(jnp.full((1, W), -r * (T * n), F32))

    def mask_of(r, lo, c):
        er = jnp.exp(-r * ucol_f[lo:])
        er = jnp.concatenate([er, er], axis=1)
        ek = jnp.exp(r * urow_f[:, c : c + HALF])
        return er * ek * keep_s[lo:, c : c + HALF]

    for h in range(H):
        load(0, h).wait()
        load(1, h).wait()
        ks = (k_s[h].astype(F32) * w_out_of(rates[h])).astype(BF16)
        st = dot(ks, v_s[h], TN).astype(BF16)
        for i in range(M):
            share_out[0, i, h] = st[i * ROWS : (i + 1) * ROWS]

    pl.semaphore_wait(barrier, M - 1 + G - 1 + NHEAD - 1)

    def share(way, k):
        to = peer(k)
        return pltpu.make_async_remote_copy(
            src_ref=share_out.at[way, to],
            dst_ref=share_in.at[way, m],
            send_sem=share_ss.at[way, k - 1],
            recv_sem=share_rs.at[way, k - 1],
            device_id=member(to),
            device_id_type=MESH,
        )

    def back(way, k):
        to = peer(k)
        return pltpu.make_async_remote_copy(
            src_ref=back_out.at[way, to],
            dst_ref=back_in.at[way, m],
            send_sem=back_ss.at[way, k - 1],
            recv_sem=back_rs.at[way, k - 1],
            device_id=member(to),
            device_id_type=MESH,
        )

    def tot(way, k):
        step = k * M if way == 0 else SEQ - k * M
        return pltpu.make_async_remote_copy(
            src_ref=tot_out.at[way],
            dst_ref=tot_in.at[way, k - 1],
            send_sem=tot_ss.at[way, k - 1],
            recv_sem=tot_rs.at[way, k - 1],
            device_id=(lax.rem(s + step, SEQ), hd),
            device_id_type=MESH,
        )

    def sends(way, k):
        return g + k < G if way == 0 else g - k >= 0

    def receives(way, k):
        return g - k >= 0 if way == 0 else g + k < G

    def start_shares(way):
        for k in range(1, M):
            share(way, k).start()
        share_in[way, m] = share_out[way, m]

    def start_totals(way):
        for k in range(1, M):
            share(way, k).wait_recv()
        one = [power(rates[h], 1.0) for h in range(H)]
        run = [jnp.zeros((ROWS, W), F32) for _ in range(H)]
        for i in range(M) if way == 0 else reversed(range(M)):
            free = clear(g * M + i, 1)
            for h in range(H):
                loc_s[i, h] = run[h]
                run[h] = run[h] * (one[h] * free) + share_in[way, i, h].astype(F32)
        for h in range(H):
            tot_out[way, h] = run[h].astype(BF16)
        for k in range(1, G):

            @pl.when(sends(way, k))
            def _():
                tot(way, k).start()

    def start_back(way):
        near = lax.rem(g + (G - 1 if way == 0 else 1), G)
        next_near = lax.rem(g + (G - 2 if way == 0 else 2), G)
        free1 = clear(near * M, M)
        free2 = free1 * clear(next_near * M, M)
        coef = [
            None,
            [power(rates[h], 1.0 * M) * free1 for h in range(H)],
            [power(rates[h], 2.0 * M) * free2 for h in range(H)],
        ]
        spread = []
        for i in range(M):
            n = i if way == 0 else M - 1 - i
            free = clear(g * M if way == 0 else g * M + i + 1, n)
            spread.append([power(rates[h], 1.0 * n) * free for h in range(H)])
        carry_s[...] = jnp.zeros_like(carry_s)
        for k in range(1, G):

            @pl.when(receives(way, k))
            def _():
                tot(way, k).wait_recv()
                for h in range(H):
                    term = tot_in[way, k - 1, h].astype(F32)
                    if k > 1:
                        term = term * coef[k - 1][h]
                    carry_s[h] = carry_s[h] + term

        for h in range(H):
            carry = carry_s[h]
            for i in range(M):
                back_out[way, i, h] = (loc_s[i, h] + carry * spread[i][h]).astype(BF16)
        for k in range(1, M):
            back(way, k).start()
        back_in[way, m] = back_out[way, m]

    def wait_back(way):
        for k in range(1, M):
            back(way, k).wait_recv()

    def finish(way):
        for k in range(1, M):
            share(way, k).wait_send()
            back(way, k).wait_send()
        for k in range(1, G):

            @pl.when(sends(way, k))
            def _():
                tot(way, k).wait_send()

    def whole(way, h):
        return back_in[way, :, h].reshape(W, W)

    def forward(h, _):
        r = rates[h]
        for c in (0, HALF):
            scores = dot(q_s[h, c:], k_s[h, c : c + HALF], NT)
            w_s[h, c:, c : c + HALF] = (scores * mask_of(r, c, c)).astype(BF16)
        att_s[h, :HALF] = dot(w_s[h, :HALF, :HALF], v_s[h, :HALF], NN)
        att_s[h, HALF:] = dot(w_s[h, HALF:], v_s[h], NN)
        qs = (q_s[h].astype(F32) * w_in_of(r)).astype(BF16)
        qt_s[h] = qs.T
        return 0

    def backward(h, _):
        r = rates[h]
        for c in (0, HALF):
            dw = dot(d_s[h, c:], v_s[h, c : c + HALF], NT)
            dw_s[c:, c : c + HALF] = (dw * mask_of(r, c, c)).astype(BF16)
        far_q = w_in_of(r) * dot(d_s[h], whole(0, h), NT)
        gq_s[h, :HALF] = (
            dot(dw_s[:HALF, :HALF], k_s[h, :HALF], NN) + far_q[:HALF]
        ).astype(BF16)
        gq_s[h, HALF:] = (dot(dw_s[HALF:], k_s[h], NN) + far_q[HALF:]).astype(BF16)
        store(0, h).start()
        dk_s[h, :HALF] = dot(dw_s[:, :HALF], q_s[h], TN)
        dk_s[h, HALF:] = dot(dw_s[HALF:, HALF:], q_s[h, HALF:], TN)
        dv_s[h, :HALF] = dot(w_s[h, :, :HALF], d_s[h], TN)
        dv_s[h, HALF:] = dot(w_s[h, HALF:, HALF:], d_s[h, HALF:], TN)
        return 0

    outs = (gq_hbm, gk_hbm, gv_hbm)
    held = (gq_s, gk_s, gv_s)

    def store(a, h):
        cols = pl.ds(pl.multiple_of(h * W, W), W)
        return pltpu.make_async_copy(held[a].at[h], outs[a].at[:, cols], out_sem.at[a, h])

    start_shares(0)
    start = jnp.full((T, W), -far, jnp.int32)
    for d in range(DOCS):
        start = jnp.where(ucol >= rel[d], rel[d], start)
    for c in range(0, T, W):
        col = lax.broadcasted_iota(jnp.int32, (T, W), 1) + c
        keep_s[:, c : c + W] = jnp.where((col >= start) & (col <= ucol), 1.0, 0.0)
    for h in range(H):
        load(2, h).wait()
    lax.fori_loop(0, 2, forward, 0)
    start_totals(0)
    lax.fori_loop(2, 4, forward, 0)
    start_back(0)
    lax.fori_loop(4, H, forward, 0)
    for h in range(H):
        load(3, h).wait()
    wait_back(0)

    squares = jnp.zeros((T, W), F32)
    dots = jnp.zeros((T, W), F32)
    for h in range(H):
        att = att_s[h] + w_in_of(rates[h]) * dot(q_s[h], whole(0, h), NN)
        att_s[h] = att
        squares = squares + att * att
        dots = dots + gain[:, h * W : (h + 1) * W] * og_s[h].astype(F32) * att

    def halves(x):
        high = x.astype(BF16)
        return [high, (x - high.astype(F32)).astype(BF16)]

    terms = jnp.concatenate(halves(squares) + halves(dots), axis=1)
    row = lax.broadcasted_iota(jnp.int32, (8, 4 * W), 0)
    lane = lax.broadcasted_iota(jnp.int32, (8, 4 * W), 1)
    pick = jnp.where((lane >= 2 * W) == (row == 1), 1.0, 0.0).astype(BF16)
    sums = dot(pick, terms, NT)
    sum_out[...] = sums[:2]

    def head_sum(k):
        return pltpu.make_async_remote_copy(
            src_ref=sum_out,
            dst_ref=sum_in.at[hd],
            send_sem=sum_ss.at[k - 1],
            recv_sem=sum_rs.at[k - 1],
            device_id=(s, lax.rem(hd + k, NHEAD)),
            device_id_type=MESH,
        )

    for k in range(1, NHEAD):
        head_sum(k).start()
    sum_in[hd] = sum_out[...]
    for k in range(1, NHEAD):
        head_sum(k).wait_recv()
    both = sum_in[0]
    for i in range(1, NHEAD):
        both = both + sum_in[i]
    inv = lax.rsqrt(both[0:1] / FEATURES + EPS)
    scale = inv * inv * inv * both[1:2] / FEATURES
    table = jnp.concatenate([inv, scale, jnp.zeros((6, T), F32)], axis=0).T
    inv = jnp.broadcast_to(table[:, 0:1], (T, W))
    scale = jnp.broadcast_to(table[:, 1:2], (T, W))

    for h in range(H):
        grad = gain[:, h * W : (h + 1) * W] * og_s[h].astype(F32)
        d_s[h] = (inv * grad - att_s[h] * scale).astype(BF16)
        gr = dot(qt_s[h], d_s[h], NN).astype(BF16)
        for i in range(M):
            share_out[1, i, h] = gr[i * ROWS : (i + 1) * ROWS]

    start_shares(1)

    for h in range(H):
        term = og_s[h].astype(F32) * att_s[h] * inv
        gain_mine[:, h * W : (h + 1) * W] = jnp.sum(term, axis=0, keepdims=True)

    def gain_a(k):
        return pltpu.make_async_remote_copy(
            src_ref=gain_mine,
            dst_ref=gain_in.at[m],
            send_sem=ga_ss.at[k - 1],
            recv_sem=ga_rs.at[k - 1],
            device_id=member(peer(k)),
            device_id_type=MESH,
        )

    def gain_b(k):
        return pltpu.make_async_remote_copy(
            src_ref=gain_tot,
            dst_ref=gain_all.at[g],
            send_sem=gb_ss.at[k - 1],
            recv_sem=gb_rs.at[k - 1],
            device_id=(lax.rem(s + k * M, SEQ), hd),
            device_id_type=MESH,
        )

    for k in range(1, M):
        gain_a(k).start()
    gain_in[m] = gain_mine[...]

    lax.fori_loop(0, 2, backward, 0)
    start_totals(1)
    for k in range(1, M):
        gain_a(k).wait_recv()
    part = gain_in[0]
    for i in range(1, M):
        part = part + gain_in[i]
    gain_tot[...] = part
    for k in range(1, G):
        gain_b(k).start()
    gain_all[g] = part
    lax.fori_loop(2, 4, backward, 0)
    start_back(1)
    lax.fori_loop(4, H, backward, 0)
    for k in range(1, G):
        gain_b(k).wait_recv()
    part = gain_all[0]
    for i in range(1, G):
        part = part + gain_all[i]
    gg_ref[...] = part * (1.0 / math.sqrt(TOKENS))
    wait_back(1)

    for h in range(H):
        w_out = w_out_of(rates[h])
        out = whole(1, h)
        gk_s[h] = (dk_s[h] + w_out * dot(v_s[h], out, NT)).astype(BF16)
        store(1, h).start()
        gv_s[h] = (dv_s[h] + w_out * dot(k_s[h], out, NN)).astype(BF16)
        store(2, h).start()

    finish(0)
    finish(1)
    for k in range(1, NHEAD):
        head_sum(k).wait_send()
    for k in range(1, M):
        gain_a(k).wait_send()
    for k in range(1, G):
        gain_b(k).wait_send()
    for a in range(3):
        for h in range(H):
            store(a, h).wait()


def on_device(queries, keys, values, doc_lengths, decay_rates, gain, out_grad):
    any_space = pl.BlockSpec(memory_space=pl.ANY)
    smem = pl.BlockSpec(memory_space=pltpu.SMEM)
    vmem = pl.BlockSpec(memory_space=pltpu.VMEM)
    block = jax.ShapeDtypeStruct((T, H * W), BF16)
    dma = pltpu.SemaphoreType.DMA
    wide = pltpu.VMEM((H, T, W), BF16)
    wide32 = pltpu.VMEM((H, T, W), F32)
    shares = pltpu.VMEM((2, M, H, ROWS, W), BF16)
    gq, gk, gv, gg = pl.pallas_call(
        kernel,
        out_shape=(block, block, block, jax.ShapeDtypeStruct((1, H * W), F32)),
        in_specs=[smem, smem, vmem, any_space, any_space, any_space, any_space],
        out_specs=(any_space, any_space, any_space, vmem),
        scratch_shapes=[
            wide,
            wide,
            wide,
            wide,
            pltpu.VMEM((H, T, T), BF16),
            pltpu.VMEM((T, T), BF16),
            pltpu.VMEM((T, T), F32),
            wide32,
            wide,
            pltpu.VMEM((H, W, T), BF16),
            wide32,
            wide32,
            wide,
            wide,
            wide,
            shares,
            shares,
            pltpu.VMEM((2, H, ROWS, W), BF16),
            pltpu.VMEM((2, G - 1, H, ROWS, W), BF16),
            pltpu.VMEM((H, ROWS, W), F32),
            pltpu.VMEM((M, H, ROWS, W), F32),
            shares,
            shares,
            pltpu.VMEM((2, T), F32),
            pltpu.VMEM((NHEAD, 2, T), F32),
            pltpu.VMEM((1, H * W), F32),
            pltpu.VMEM((M, 1, H * W), F32),
            pltpu.VMEM((1, H * W), F32),
            pltpu.VMEM((G, 1, H * W), F32),
            dma((4, H)),
            dma((3, H)),
            dma((2, M - 1)),
            dma((2, M - 1)),
            dma((2, G - 1)),
            dma((2, G - 1)),
            dma((2, M - 1)),
            dma((2, M - 1)),
            dma((NHEAD - 1,)),
            dma((NHEAD - 1,)),
            dma((M - 1,)),
            dma((M - 1,)),
            dma((G - 1,)),
            dma((G - 1,)),
        ],
        compiler_params=pltpu.CompilerParams(
            collective_id=0, has_side_effects=True, vmem_limit_bytes=48 << 20
        ),
        cost_estimate=pl.CostEstimate(
            flops=2 * H * (6 * T * T * W + 6 * T * W * W),
            bytes_accessed=7 * T * H * W * 2,
            transcendentals=4 * H * T * W,
        ),
    )(doc_lengths, decay_rates, gain.reshape(1, H * W), queries, keys, values, out_grad)
    return gq, gk, gv, gg.reshape(H * W)


def solution(mesh):
    return jax.shard_map(
        on_device,
        mesh=mesh,
        in_specs=(
            P("seq", "head"),
            P("seq", "head"),
            P("seq", "head"),
            P(),
            P("head"),
            P("head"),
            P("seq", "head"),
        ),
        out_specs=(P("seq", "head"), P("seq", "head"), P("seq", "head"), P("head")),
        check_vma=False,
    )
```

time: 344 us -> 58.1 us (0.17); the launches traced: 340 us -> 57.8 us
  waiting for transfers between devices: 107 us -> 0 us
  blocking collectives: 101 us -> 0 us
  Pallas kernels: 0 us -> 48.7 us
  other arithmetic: 40.4 us -> 0.61 us
  local copies, waits for them, and re-layouts: 46.1 us -> 7.87 us
  matrix products: 28.7 us -> 0 us
  between operations: 16.5 us -> 0.67 us
    all_gather x2 -> x0, waiting for transfers between devices: 107 us -> none  [the longest x1 81.1 us: on_device(): piece = lax.all_gather(states[None], 'seq', axis=0, tiled=True)]
    unnamed x1 -> x0, blocking collectives: 74.3 us -> none
    pallas_call x0 -> x1, Pallas kernels: none -> 48.7 us  [on_device(): pl.pallas_call(kernel, out_shape=(block, block, block, jax.ShapeDtypeStru...]
    select_n x32 -> x0, other arithmetic: 34.4 us -> none  [the longest x31 34.4 us: lap(): jnp.where(position < mine, new, old)]
    dot_general x13 -> x0, matrix products: 28.7 us -> none  [the longest x1 9.02 us: on_device(): jnp.einsum('nh,nhab->hab', factor, piece.astype(jnp.float32), precision=l...]
    psum x2 -> x0, blocking collectives: 26.6 us -> none  [on_device(): lax.psum((jnp.sum(flat * flat, axis=1), jnp.sum(scaled_grad * flat, axis=...]
    mul x31 -> x0, local copies, waits for them, and re-layouts: 21.3 us -> none  [chain_combine(): earlier[1] * later[0][:, None, None] + later[1]]
    rev x2 -> x0, local copies, waits for them, and re-layouts: 11.9 us -> none  [prefix(): pieces = jax.tree.map(lambda part: part[::-1], pieces)]
  transfers between devices with their start and end apart: 2 -> 0, of which waited for: 2 -> 0; matrix products, arithmetic and copies ran while one was open for 6% -> 0% of each run, Pallas kernels for 0% -> 0%
where the time goes in v1:
time: 58.1 us; the launch traced here: 57.8 us
  Pallas kernels  48.7 us (84%)
  local copies, waits for them, and re-layouts  7.87 us (14%)
  between operations  0.67 us (1%)
  other arithmetic  0.61 us (1%)
    pallas_call x1, Pallas kernels, on_device(): pl.pallas_call(kernel, out_shape=(block, block, block, jax.ShapeDtypeStru...  48.7 us
    unnamed x15, local copies, waits for them, and re-layouts  7.17 us

profile of v1, /device:TPU:2, one launch (start us, length us, event | category | flops | bytes accessed | tf_op | source)
XLA Modules:
  0.0 57.8 jit_solution(8328920344605617427)
XLA Ops:
  0.6 0.0 copy-start.4
  0.6 0.0 copy-start.5
  0.7 0.7 %reshape.14.gain = f32[1,768]{1,0:T(1,128)S(1)} reshape(f32[768]{0:T(1024)} %param.12) | data formatting | bytes 6144 | tf_op jit(solution)/shard_map/reshape | solution.py:538
  1.4 0.0 copy-done.4
  1.4 0.0 copy-done.5
  1.4 0.0 copy-start
  1.4 1.1 %copy-done = bf16[512,768]{1,0:T(8,128)(2,1)S(1)} copy-done((bf16[512,768]{1,0:T(8,128)(2,1)S(1)}, bf16[512,768]{1,0:T(8,128)(2,1)}, u32[]{:S(2)}) %copy-start) | copy-done | bytes 786456
  2.5 0.0 copy-start.1
  2.5 1.1 %copy-done.1 = bf16[512,768]{1,0:T(8,128)(2,1)S(1)} copy-done((bf16[512,768]{1,0:T(8,128)(2,1)S(1)}, bf16[512,768]{1,0:T(8,128)(2,1)}, u32[]{:S(2)}) %copy-start.1) | copy-done | bytes 786456
  3.6 0.0 copy-start.2
  3.6 1.1 %copy-done.2 = bf16[512,768]{1,0:T(8,128)(2,1)S(1)} copy-done((bf16[512,768]{1,0:T(8,128)(2,1)S(1)}, bf16[512,768]{1,0:T(8,128)(2,1)}, u32[]{:S(2)}) %copy-start.2) | copy-done | bytes 786456
  4.8 0.0 copy-start.3
  4.8 1.1 %copy-done.3 = bf16[512,768]{1,0:T(8,128)(2,1)S(1)} copy-done((bf16[512,768]{1,0:T(8,128)(2,1)S(1)}, bf16[512,768]{1,0:T(8,128)(2,1)}, u32[]{:S(2)}) %copy-start.3) | copy-done | bytes 786456
  5.9 48.7 %shard_map.102 = (bf16[512,768]{1,0:T(8,128)(2,1)S(1)}, bf16[512,768]{1,0:T(8,128)(2,1)S(1)}, bf16[512,768]{1,0:T(8,128)(2,1)S(1)}, f32[1,768]{1,0:T(1,128)S(1)}) custom-call(s32[32]{0:T(128)S(1)} %copy-done.4, f32[6]{0:T(128)S(1)} %copy-done.5, f32[1,768]{1,0:T(1,128)S(1)} %reshape.14.gain, bf16[512,768]{1,0:T(8,128)(2,1)S(1)} %copy-done, ...), custom_call_target="tpu_custom_call" | custom-call | flops 3019898880 | bytes 5505024 | tf_op jit(solution)/shard_map/pallas_call | solution.py:480
  54.6 0.6 %reduce = f32[768]{0:T(1024)} reduce(f32[1,768]{1,0:T(1,128)S(1)} %get-tuple-element.11, f32[]{:T(128)} %constant.1), dimensions={0}, to_apply=%get-tuple-element.11.reduce_sub_computation | reduce | bytes 6148 | tf_op jit(solution)/shard_map/pallas_call | solution.py:480
  55.2 0.9 %copy.14 = bf16[512,768]{1,0:T(8,128)(2,1)} copy(bf16[512,768]{1,0:T(8,128)(2,1)S(1)} %get-tuple-element.16) | data formatting | bytes 1572864
  56.1 0.9 %copy.15 = bf16[512,768]{1,0:T(8,128)(2,1)} copy(bf16[512,768]{1,0:T(8,128)(2,1)S(1)} %get-tuple-element.17) | data formatting | bytes 1572864
  57.0 0.9 %copy.16 = bf16[512,768]{1,0:T(8,128)(2,1)} copy(bf16[512,768]{1,0:T(8,128)(2,1)S(1)} %get-tuple-element.18) | data formatting | bytes 1572864
Async XLA Ops:
  0.6 0.7 %copy-start.4 = (s32[32]{0:T(128)S(1)}, s32[32]{0:T(128)}, u32[]{:S(2)}) copy-start(s32[32]{0:T(128)} %docs.1) | copy-start | bytes 388
  0.6 0.7 %copy-start.5 = (f32[6]{0:T(128)S(1)}, f32[6]{0:T(128)}, u32[]{:S(2)}) copy-start(f32[6]{0:T(128)} %rates.1) | copy-start | bytes 76
  1.4 1.1 %copy-start = (bf16[512,768]{1,0:T(8,128)(2,1)S(1)}, bf16[512,768]{1,0:T(8,128)(2,1)}, u32[]{:S(2)}) copy-start(bf16[512,768]{1,0:T(8,128)(2,1)} %q_hbm.1) | copy-start | bytes 2359300
  2.5 1.1 %copy-start.1 = (bf16[512,768]{1,0:T(8,128)(2,1)S(1)}, bf16[512,768]{1,0:T(8,128)(2,1)}, u32[]{:S(2)}) copy-start(bf16[512,768]{1,0:T(8,128)(2,1)} %k_hbm.1) | copy-start | bytes 2359300
  3.6 1.1 %copy-start.2 = (bf16[512,768]{1,0:T(8,128)(2,1)S(1)}, bf16[512,768]{1,0:T(8,128)(2,1)}, u32[]{:S(2)}) copy-start(bf16[512,768]{1,0:T(8,128)(2,1)} %v_hbm.1) | copy-start | bytes 2359300
  4.8 1.1 %copy-start.3 = (bf16[512,768]{1,0:T(8,128)(2,1)S(1)}, bf16[512,768]{1,0:T(8,128)(2,1)}, u32[]{:S(2)}) copy-start(bf16[512,768]{1,0:T(8,128)(2,1)} %og_hbm.1) | copy-start | bytes 2359300

commit v2 on v1

v2 whole, which is shorter than its diff:
```python
import math

import jax
import jax.numpy as jnp
from jax import lax
from jax.experimental import pallas as pl
from jax.experimental.pallas import tpu as pltpu
from jax.sharding import PartitionSpec as P

EPS = 1e-06
MESH = pl.DeviceIdType.MESH
F32 = jnp.float32
BF16 = jnp.bfloat16
NT = (((1,), (1,)), ((), ()))
TN = (((0,), (0,)), ((), ()))
NN = (((1,), (0,)), ((), ()))

T = 512
HALF = T // 2
W = 128
H = 6
FEATURES = 6144
TOKENS = 16384
SEQ = 32
M = 8
G = SEQ // M
NX = 4
OFFSETS = ((1, 2), (1, 1), (1, 3), (1, 0), (0, 2), (0, 1), (0, 3))
FAR_FIRST = (2, 3, 1)
PARTS = 2
HB = H // PARTS
ROWS = W // M
NHEAD = 8
DOCS = 32


def dot(a, b, dims):
    return lax.dot_general(a, b, dims, preferred_element_type=F32)


def kernel(
    docs,
    rates,
    gain,
    q_hbm,
    k_hbm,
    v_hbm,
    og_hbm,
    gq_s,
    gk_s,
    gv_s,
    gg_ref,
    q_s,
    k_s,
    v_s,
    og_s,
    w_s,
    dw_s,
    keep_s,
    wi_s,
    wo_s,
    g_s,
    dk_s,
    dv_s,
    att_s,
    d_s,
    qt_s,
    inc_s,
    squares_s,
    dots_s,
    one_s,
    coef_s,
    spread_s,
    share_out,
    share_in,
    tot_out,
    tot_in,
    carry_s,
    loc_s,
    back_out,
    back_in,
    sum_out,
    sum_in,
    gain_mine,
    gain_in,
    gain_tot,
    gain_all,
    in_sem,
    share_ss,
    share_rs,
    tot_ss,
    tot_rs,
    back_ss,
    back_rs,
    sum_ss,
    sum_rs,
    ga_ss,
    ga_rs,
    gb_ss,
    gb_rs,
):
    s = lax.axis_index("seq")
    hd = lax.axis_index("head")
    g = s // M
    m = lax.rem(s, M)

    def member(i):
        return (g * M + i, hd)

    def peer(o):
        dz, dx = OFFSETS[o]
        return lax.rem(m // NX + dz, 2) * NX + lax.rem(lax.rem(m, NX) + dx, NX)

    def place(group, i):
        return lax.rem(i + jnp.where(group >= G // 2, NX, 0), M)

    mine = place(g, m)

    def ally(k):
        other = lax.rem(g + k, G)
        return (other * M + place(other, mine), hd)

    barrier = pltpu.get_barrier_semaphore()
    for o in range(M - 1):
        pl.semaphore_signal(barrier, inc=1, device_id=member(peer(o)), device_id_type=MESH)
    for k in range(1, G):
        pl.semaphore_signal(barrier, inc=1, device_id=ally(k), device_id_type=MESH)
    for k in range(1, NHEAD):
        pl.semaphore_signal(
            barrier, inc=1, device_id=(s, lax.rem(hd + k, NHEAD)), device_id_type=MESH
        )

    hbm = (k_hbm, v_hbm, q_hbm, og_hbm)
    vmem = (k_s, v_s, q_s, og_s)

    def load(a, h):
        return pltpu.make_async_copy(
            hbm[a].at[:, h * W : (h + 1) * W], vmem[a].at[h], in_sem.at[a, h]
        )

    for h in range(H):
        load(0, h).start()
        load(1, h).start()
    for h in range(H):
        load(2, h).start()
        load(3, h).start()

    begin = s * T
    far = jnp.int32(1 << 24)
    total = jnp.int32(0)
    bits = jnp.int32(0)
    first_end = far
    last_start = -far
    rel = []
    for d in range(DOCS):
        total = total + docs[d]
        here = total - begin
        rel.append(here)
        if d < DOCS - 1:
            bits = bits | lax.shift_left(jnp.int32(1), lax.shift_right_logical(total, 9))
        first_end = jnp.where((here >= 0) & (first_end == far), here, first_end)
        last_start = jnp.where(here <= T - 1, here, last_start)

    def clear(at, count):
        if count == 0:
            return jnp.float32(1.0)
        field = lax.shift_right_logical(bits, at) & jnp.int32((1 << count) - 1)
        return jnp.where(field == 0, jnp.float32(1.0), jnp.float32(0.0))

    ucol = lax.broadcasted_iota(jnp.int32, (T, W), 0)
    ucol_f = ucol.astype(F32)
    urow_f = lax.broadcasted_iota(jnp.int32, (1, T), 1).astype(F32)

    def mask_of(r, lo, c):
        er = jnp.exp(-r * ucol_f[lo:])
        er = jnp.concatenate([er, er], axis=1)
        ek = jnp.exp(r * urow_f[:, c : c + HALF])
        return er * ek * keep_s[lo:, c : c + HALF]

    def share(way, b, o):
        to = peer(o)
        return pltpu.make_async_remote_copy(
            src_ref=share_out.at[way, b, place(g, to)],
            dst_ref=share_in.at[way, b, m],
            send_sem=share_ss.at[way, b, o],
            recv_sem=share_rs.at[way, b, o],
            device_id=member(to),
            device_id_type=MESH,
        )

    def back(way, b, o):
        to = peer(o)
        return pltpu.make_async_remote_copy(
            src_ref=back_out.at[way, b, to],
            dst_ref=back_in.at[way, b, mine],
            send_sem=back_ss.at[way, b, o],
            recv_sem=back_rs.at[way, b, o],
            device_id=member(to),
            device_id_type=MESH,
        )

    def tot(way, b, k):
        return pltpu.make_async_remote_copy(
            src_ref=tot_out.at[way, b],
            dst_ref=tot_in.at[way, b, k - 1],
            send_sem=tot_ss.at[way, b, k - 1],
            recv_sem=tot_rs.at[way, b, k - 1],
            device_id=ally(k if way == 0 else G - k),
            device_id_type=MESH,
        )

    def sends(way, k):
        return g + k < G if way == 0 else g - k >= 0

    def receives(way, k):
        return g - k >= 0 if way == 0 else g + k < G

    def start_shares(way, b):
        for o in range(M - 1):
            share(way, b, o).start()
        share_in[way, b, m] = share_out[way, b, mine]

    def start_totals(way, b):
        for o in reversed(range(M - 1)):
            share(way, b, o).wait_recv()
        run = [jnp.zeros((ROWS, W), F32) for _ in range(HB)]
        for i in range(M) if way == 0 else reversed(range(M)):
            for e in range(HB):
                h = b * HB + e
                loc_s[b, i, e] = run[e]
                run[e] = run[e] * one_s[i, h : h + 1] + share_in[way, b, i, e].astype(F32)
        for e in range(HB):
            tot_out[way, b, e] = run[e].astype(BF16)
        for k in FAR_FIRST:

            @pl.when(sends(way, k))
            def _():
                tot(way, b, k).start()

    def start_back(way, b):
        carry_s[b] = jnp.zeros((HB, ROWS, W), F32)
        for k in reversed(FAR_FIRST):

            @pl.when(receives(way, k))
            def _():
                tot(way, b, k).wait_recv()
                for e in range(HB):
                    h = b * HB + e
                    term = tot_in[way, b, k - 1, e].astype(F32)
                    if k > 1:
                        term = term * coef_s[way, k - 2, h : h + 1]
                    carry_s[b, e] = carry_s[b, e] + term

        for e in range(HB):
            h = b * HB + e
            carry = carry_s[b, e]
            for i in range(M):
                back_out[way, b, i, e] = (
                    loc_s[b, i, e] + carry * spread_s[way, i, h : h + 1]
                ).astype(BF16)
        for o in range(M - 1):
            back(way, b, o).start()
        back_in[way, b, mine] = back_out[way, b, m]

    def wait_back(way, b):
        for o in reversed(range(M - 1)):
            back(way, b, o).wait_recv()

    def whole(way, b, e):
        return back_in[way, b, :, e].reshape(W, W)

    def forward(h, _):
        r = rates[h]
        for c in (0, HALF):
            scores = dot(q_s[h, c:], k_s[h, c : c + HALF], NT)
            w_s[h, c:, c : c + HALF] = (scores * mask_of(r, c, c)).astype(BF16)
        att_s[h, :HALF] = dot(w_s[h, :HALF, :HALF], v_s[h, :HALF], NN)
        att_s[h, HALF:] = dot(w_s[h, HALF:], v_s[h], NN)
        w_in = jnp.where(ucol < first_end, jnp.exp(-r * (ucol_f + 1.0)), 0.0)
        wi_s[h] = w_in
        qt_s[h] = (q_s[h].astype(F32) * w_in).astype(BF16).T
        return 0

    def backward(h, _):
        r = rates[h]
        for c in (0, HALF):
            dw = dot(d_s[h, c:], v_s[h, c : c + HALF], NT)
            dw_s[c:, c : c + HALF] = (dw * mask_of(r, c, c)).astype(BF16)
        far_q = wi_s[h] * dot(d_s[h], inc_s[h], NT)
        cols = pl.ds(pl.multiple_of(h * W, W), W)
        gq_s[:HALF, cols] = (
            dot(dw_s[:HALF, :HALF], k_s[h, :HALF], NN) + far_q[:HALF]
        ).astype(BF16)
        gq_s[HALF:, cols] = (dot(dw_s[HALF:], k_s[h], NN) + far_q[HALF:]).astype(BF16)
        dk_s[h, :HALF] = dot(dw_s[:, :HALF], q_s[h], TN)
        dk_s[h, HALF:] = dot(dw_s[HALF:, HALF:], q_s[h, HALF:], TN)
        dv_s[h, :HALF] = dot(w_s[h, :, :HALF], d_s[h], TN)
        dv_s[h, HALF:] = dot(w_s[h, HALF:, HALF:], d_s[h, HALF:], TN)
        return 0

    for b in range(PARTS):
        for e in range(HB):
            h = b * HB + e
            load(0, h).wait()
            load(1, h).wait()
            w_out = jnp.where(
                ucol >= last_start, jnp.exp(-rates[h] * (T - 1.0 - ucol_f)), 0.0
            )
            wo_s[h] = w_out
            ks = (k_s[h].astype(F32) * w_out).astype(BF16)
            st = dot(ks, v_s[h], TN).astype(BF16)
            for i in range(M):
                share_out[0, b, i, e] = st[i * ROWS : (i + 1) * ROWS]
        if b == 0:
            pl.semaphore_wait(barrier, M - 1 + G - 1 + NHEAD - 1)
        start_shares(0, b)

    row = lax.broadcasted_iota(jnp.int32, (8, W), 0)
    rate_rows = jnp.zeros((8, W), F32)
    for h in range(H):
        rate_rows = jnp.where(row == h, rates[h], rate_rows)

    def power(n):
        return jnp.exp(rate_rows * (-float(T) * n))

    for i in range(M):
        one_s[i] = power(1) * clear(g * M + i, 1)
        spread_s[0, i] = power(i) * clear(g * M, i)
        spread_s[1, i] = power(M - 1 - i) * clear(g * M + i + 1, M - 1 - i)
    for way in range(2):
        near = lax.rem(g + (G - 1 if way == 0 else 1), G)
        next_near = lax.rem(g + (G - 2 if way == 0 else 2), G)
        free = clear(near * M, M)
        coef_s[way, 0] = power(M) * free
        coef_s[way, 1] = power(2 * M) * (free * clear(next_near * M, M))

    start = jnp.full((T, W), -far, jnp.int32)
    for d in range(DOCS):
        start = jnp.where(ucol >= rel[d], rel[d], start)
    for c in range(0, T, W):
        col = lax.broadcasted_iota(jnp.int32, (T, W), 1) + c
        keep_s[:, c : c + W] = jnp.where((col >= start) & (col <= ucol), 1.0, 0.0)
    for h in range(H):
        load(2, h).wait()
        load(3, h).wait()
        g_s[h] = gain[:, h * W : (h + 1) * W] * og_s[h].astype(F32)
    lax.fori_loop(0, 3, forward, 0)
    for b in range(PARTS):
        start_totals(0, b)
    lax.fori_loop(3, H, forward, 0)
    for b in range(PARTS):
        start_back(0, b)

    squares_s[...] = jnp.zeros_like(squares_s)
    dots_s[...] = jnp.zeros_like(dots_s)
    for b in range(PARTS):
        wait_back(0, b)
        for e in range(HB):
            h = b * HB + e
            inc = whole(0, b, e)
            inc_s[h] = inc
            att = att_s[h] + wi_s[h] * dot(q_s[h], inc, NN)
            att_s[h] = att
            squares_s[...] += att * att
            dots_s[...] += g_s[h] * att

    def halves(x):
        high = x.astype(BF16)
        return [high, (x - high.astype(F32)).astype(BF16)]

    terms = jnp.concatenate(halves(squares_s[...]) + halves(dots_s[...]), axis=1)
    row = lax.broadcasted_iota(jnp.int32, (8, 4 * W), 0)
    lane = lax.broadcasted_iota(jnp.int32, (8, 4 * W), 1)
    pick = jnp.where((lane >= 2 * W) == (row == 1), 1.0, 0.0).astype(BF16)
    sums = dot(pick, terms, NT)
    sum_out[...] = sums[:2]

    def head_sum(k):
        return pltpu.make_async_remote_copy(
            src_ref=sum_out,
            dst_ref=sum_in.at[hd],
            send_sem=sum_ss.at[k - 1],
            recv_sem=sum_rs.at[k - 1],
            device_id=(s, lax.rem(hd + k, NHEAD)),
            device_id_type=MESH,
        )

    for k in range(1, NHEAD):
        head_sum(k).start()
    sum_in[hd] = sum_out[...]
    for k in range(1, NHEAD):
        head_sum(k).wait_recv()
    both = sum_in[0]
    for i in range(1, NHEAD):
        both = both + sum_in[i]
    inv = lax.rsqrt(both[0:1] / FEATURES + EPS)
    scale = inv * inv * inv * both[1:2] / FEATURES
    table = jnp.concatenate([inv, scale, jnp.zeros((6, T), F32)], axis=0).T
    inv = jnp.broadcast_to(table[:, 0:1], (T, W))
    scale = jnp.broadcast_to(table[:, 1:2], (T, W))

    for b in range(PARTS):
        for e in range(HB):
            h = b * HB + e
            d_s[h] = (inv * g_s[h] - att_s[h] * scale).astype(BF16)
            gr = dot(qt_s[h], d_s[h], NN).astype(BF16)
            for i in range(M):
                share_out[1, b, i, e] = gr[i * ROWS : (i + 1) * ROWS]
        start_shares(1, b)

    for h in range(H):
        term = og_s[h].astype(F32) * att_s[h] * inv
        gain_mine[:, h * W : (h + 1) * W] = jnp.sum(term, axis=0, keepdims=True)

    def gain_a(o):
        return pltpu.make_async_remote_copy(
            src_ref=gain_mine,
            dst_ref=gain_in.at[m],
            send_sem=ga_ss.at[o],
            recv_sem=ga_rs.at[o],
            device_id=member(peer(o)),
            device_id_type=MESH,
        )

    def gain_b(k):
        return pltpu.make_async_remote_copy(
            src_ref=gain_tot,
            dst_ref=gain_all.at[g],
            send_sem=gb_ss.at[k - 1],
            recv_sem=gb_rs.at[k - 1],
            device_id=ally(k),
            device_id_type=MESH,
        )

    for o in range(M - 1):
        gain_a(o).start()
    gain_in[m] = gain_mine[...]

    lax.fori_loop(0, 3, backward, 0)
    for b in range(PARTS):
        start_totals(1, b)
    for o in range(M - 1):
        gain_a(o).wait_recv()
    part = gain_in[0]
    for i in range(1, M):
        part = part + gain_in[i]
    gain_tot[...] = part
    for k in range(1, G):
        gain_b(k).start()
    gain_all[g] = part
    lax.fori_loop(3, H, backward, 0)
    for b in range(PARTS):
        start_back(1, b)
    for k in range(1, G):
        gain_b(k).wait_recv()
    part = gain_all[0]
    for i in range(1, G):
        part = part + gain_all[i]
    gg_ref[...] = part * (1.0 / math.sqrt(TOKENS))

    for b in range(PARTS):
        for o in range(M - 1):
            share(0, b, o).wait_send()
            back(0, b, o).wait_send()
            share(1, b, o).wait_send()
        for k in range(1, G):
            for way in range(2):

                @pl.when(sends(way, k))
                def _():
                    tot(way, b, k).wait_send()

    for k in range(1, NHEAD):
        head_sum(k).wait_send()
    for o in range(M - 1):
        gain_a(o).wait_send()
    for k in range(1, G):
        gain_b(k).wait_send()

    for b in range(PARTS):
        wait_back(1, b)
        for e in range(HB):
            h = b * HB + e
            out = whole(1, b, e)
            gk_s[:, h * W : (h + 1) * W] = (dk_s[h] + wo_s[h] * dot(v_s[h], out, NT)).astype(BF16)
            gv_s[:, h * W : (h + 1) * W] = (dv_s[h] + wo_s[h] * dot(k_s[h], out, NN)).astype(BF16)
    for b in range(PARTS):
        for o in range(M - 1):
            back(1, b, o).wait_send()


def write(gq_s, gk_s, gv_s, gg_s, gq_hbm, gk_hbm, gv_hbm, gg_ref, sem):
    held = (gq_s, gk_s, gv_s)
    outs = (gq_hbm, gk_hbm, gv_hbm)

    def store(a, c):
        rows = slice(c * W, (c + 1) * W)
        return pltpu.make_async_copy(held[a].at[rows], outs[a].at[rows], sem.at[a, c])

    for a in range(3):
        for c in range(T // W):
            store(a, c).start()
    for h in range(H):
        gg_ref[h * W : (h + 1) * W] = gg_s[0, h * W : (h + 1) * W]
    for a in range(3):
        for c in range(T // W):
            store(a, c).wait()


def on_device(queries, keys, values, doc_lengths, decay_rates, gain, out_grad):
    hbm = pl.BlockSpec(memory_space=pltpu.HBM)
    smem = pl.BlockSpec(memory_space=pltpu.SMEM)
    vmem = pl.BlockSpec(memory_space=pltpu.VMEM)
    dma = pltpu.SemaphoreType.DMA
    wide = (H, T, W)
    shares = pltpu.VMEM((2, PARTS, M, HB, ROWS, W), BF16)
    block = jax.ShapeDtypeStruct((T, H * W), BF16)
    row = jax.ShapeDtypeStruct((1, H * W), F32)
    gq, gk, gv, gg = pl.pallas_call(
        kernel,
        out_shape=(
            block,
            block,
            block,
            row,
        ),
        in_specs=[smem, smem, vmem, hbm, hbm, hbm, hbm],
        out_specs=(vmem,) * 4,
        scratch_shapes=[
            pltpu.VMEM(wide, BF16),
            pltpu.VMEM(wide, BF16),
            pltpu.VMEM(wide, BF16),
            pltpu.VMEM(wide, BF16),
            pltpu.VMEM((H, T, T), BF16),
            pltpu.VMEM((T, T), BF16),
            pltpu.VMEM((T, T), F32),
            pltpu.VMEM(wide, F32),
            pltpu.VMEM(wide, F32),
            pltpu.VMEM(wide, F32),
            pltpu.VMEM(wide, F32),
            pltpu.VMEM(wide, F32),
            pltpu.VMEM(wide, F32),
            pltpu.VMEM(wide, BF16),
            pltpu.VMEM((H, W, T), BF16),
            pltpu.VMEM((H, W, W), BF16),
            pltpu.VMEM((T, W), F32),
            pltpu.VMEM((T, W), F32),
            pltpu.VMEM((M, 8, W), F32),
            pltpu.VMEM((2, 2, 8, W), F32),
            pltpu.VMEM((2, M, 8, W), F32),
            shares,
            shares,
            pltpu.VMEM((2, PARTS, HB, ROWS, W), BF16),
            pltpu.VMEM((2, PARTS, G - 1, HB, ROWS, W), BF16),
            pltpu.VMEM((PARTS, HB, ROWS, W), F32),
            pltpu.VMEM((PARTS, M, HB, ROWS, W), F32),
            shares,
            shares,
            pltpu.VMEM((2, T), F32),
            pltpu.VMEM((NHEAD, 2, T), F32),
            pltpu.VMEM((1, H * W), F32),
            pltpu.VMEM((M, 1, H * W), F32),
            pltpu.VMEM((1, H * W), F32),
            pltpu.VMEM((G, 1, H * W), F32),
            dma((4, H)),
            dma((2, PARTS, M - 1)),
            dma((2, PARTS, M - 1)),
            dma((2, PARTS, G - 1)),
            dma((2, PARTS, G - 1)),
            dma((2, PARTS, M - 1)),
            dma((2, PARTS, M - 1)),
            dma((NHEAD - 1,)),
            dma((NHEAD - 1,)),
            dma((M - 1,)),
            dma((M - 1,)),
            dma((G - 1,)),
            dma((G - 1,)),
        ],
        compiler_params=pltpu.CompilerParams(
            collective_id=0, has_side_effects=True, vmem_limit_bytes=51 << 20
        ),
        cost_estimate=pl.CostEstimate(
            flops=2 * H * (6 * T * T * W + 5 * T * W * W),
            bytes_accessed=4 * T * H * W * 2,
            transcendentals=4 * H * T * W,
        ),
    )(doc_lengths, decay_rates, gain.reshape(1, H * W), queries, keys, values, out_grad)
    gq, gk, gv, gg = pl.pallas_call(
        write,
        out_shape=(block, block, block, jax.ShapeDtypeStruct((H * W,), F32)),
        in_specs=[vmem] * 4,
        out_specs=(hbm, hbm, hbm, vmem),
        scratch_shapes=[dma((3, T // W))],
        compiler_params=pltpu.CompilerParams(vmem_limit_bytes=51 << 20),
        cost_estimate=pl.CostEstimate(
            flops=0, bytes_accessed=3 * T * H * W * 2, transcendentals=0
        ),
    )(gq, gk, gv, gg)
    return gq, gk, gv, gg


def solution(mesh):
    return jax.shard_map(
        on_device,
        mesh=mesh,
        in_specs=(
            P("seq", "head"),
            P("seq", "head"),
            P("seq", "head"),
            P(),
            P("head"),
            P("head"),
            P("seq", "head"),
        ),
        out_specs=(P("seq", "head"), P("seq", "head"), P("seq", "head"), P("head")),
        check_vma=False,
    )
```

time: 58.1 us -> 45.8 us (0.79)
  local copies, waits for them, and re-layouts: 7.87 us -> 0.71 us
  Pallas kernels: 48.7 us -> 44.4 us
  other arithmetic: 0.61 us -> 0 us
    unnamed x15 -> x4, local copies, waits for them, and re-layouts: 7.17 us -> 0.01 us
    pallas_call x1 -> x2, Pallas kernels: 48.7 us -> 44.4 us  [the longest x1 42.3 us: on_device(): pl.pallas_call(kernel, out_shape=(block, block, block, row), in_specs=[sm...]
    pallas_call x1 -> x0, other arithmetic: 0.61 us -> none  [on_device(): pl.pallas_call(kernel, out_shape=(block, block, block, jax.ShapeDtypeStru...]
where the time goes in v2:
time: 45.8 us; the launch traced here: 45.7 us
  Pallas kernels  44.4 us (97%)
  local copies, waits for them, and re-layouts  0.71 us (2%)
  between operations  0.66 us (1%)
    pallas_call x1, Pallas kernels, on_device(): pl.pallas_call(kernel, out_shape=(block, block, block, row), in_specs=[sm...  42.3 us
    pallas_call x1, Pallas kernels, on_device(): pl.pallas_call(write, out_shape=(block, block, block, jax.ShapeDtypeStruc...  2.07 us

profile of v2, /device:TPU:2, one launch (start us, length us, event | category | flops | bytes accessed | tf_op | source)
XLA Modules:
  0.0 45.7 jit_solution(15074166626401882928)
XLA Ops:
  0.6 0.0 copy-start.1
  0.6 0.0 copy-start
  0.7 0.7 %reshape.11.gain = f32[1,768]{1,0:T(1,128)S(1)} reshape(f32[768]{0:T(1024)} %param.12) | data formatting | bytes 6144 | tf_op jit(solution)/shard_map/reshape | solution.py:587
  1.4 0.0 copy-done.1
  1.4 0.0 copy-done
  1.4 42.3 %shard_map.102 = (bf16[512,768]{1,0:T(8,128)(2,1)S(1)}, bf16[512,768]{1,0:T(8,128)(2,1)S(1)}, bf16[512,768]{1,0:T(8,128)(2,1)S(1)}, f32[1,768]{1,0:T(1,128)S(1)}) custom-call(s32[32]{0:T(128)S(1)} %copy-done, f32[6]{0:T(128)S(1)} %copy-done.1, f32[1,768]{1,0:T(1,128)S(1)} %reshape.11.gain, bf16[512,768]{1,0:T(8,128)(2,1)} %q_hbm.1, bf16[512,768]{1,0:T(8,128)(2,1)} %k_hbm.1, ...), custom_call_target="tpu_custom_call" | custom-call | flops 2919235584 | bytes 3145728 | tf_op jit(solution)/shard_map/pallas_call | solution.py:519
  43.6 2.1 %shard_map.103 = (bf16[512,768]{1,0:T(8,128)(2,1)}, bf16[512,768]{1,0:T(8,128)(2,1)}, bf16[512,768]{1,0:T(8,128)(2,1)}, f32[768]{0:T(1024)}) custom-call(bf16[512,768]{1,0:T(8,128)(2,1)S(1)} %get-tuple-element.8.gq_s, bf16[512,768]{1,0:T(8,128)(2,1)S(1)} %get-tuple-element.9.gk_s, bf16[512,768]{1,0:T(8,128)(2,1)S(1)} %get-tuple-element.10.gv_s, ...), custom_call_target="tpu_custom_call" | custom-call | bytes 2359296 | tf_op jit(solution)/shard_map/pallas_call | solution.py:588
Async XLA Ops:
  0.6 0.7 %copy-start.1 = (f32[6]{0:T(128)S(1)}, f32[6]{0:T(128)}, u32[]{:S(2)}) copy-start(f32[6]{0:T(128)} %rates.1) | copy-start | bytes 76
  0.6 0.7 %copy-start = (s32[32]{0:T(128)S(1)}, s32[32]{0:T(128)}, u32[]{:S(2)}) copy-start(s32[32]{0:T(128)} %docs.1) | copy-start | bytes 388

commit v3 on v2

--- a/solution.py
+++ b/solution.py
@@ -27,8 +27,9 @@
 NX = 4
 OFFSETS = ((1, 2), (1, 1), (1, 3), (1, 0), (0, 2), (0, 1), (0, 3))
 FAR_FIRST = (2, 3, 1)
+OUT_PARTS = (((0, 4), (4, 6)), ((0, 4), (4, 6)))
+BACK_PARTS = (((0, 4), (4, 6)), ((0, 4), (4, 6)))
 PARTS = 2
-HB = H // PARTS
 ROWS = W // M
 NHEAD = 8
 DOCS = 32
@@ -39,9 +40,9 @@
 
 
 def kernel(
-    docs,
-    rates,
-    gain,
+    docs_hbm,
+    rates_hbm,
+    gain_hbm,
     q_hbm,
     k_hbm,
     v_hbm,
@@ -85,6 +86,10 @@
     gain_in,
     gain_tot,
     gain_all,
+    docs,
+    rates,
+    gain,
+    small_sem,
     in_sem,
     share_ss,
     share_rs,
@@ -138,6 +143,12 @@
             hbm[a].at[:, h * W : (h + 1) * W], vmem[a].at[h], in_sem.at[a, h]
         )
 
+    small = [
+        pltpu.make_async_copy(src, dst, small_sem.at[i])
+        for i, (src, dst) in enumerate(((docs_hbm, docs), (rates_hbm, rates), (gain_hbm, gain)))
+    ]
+    for copy in small:
+        copy.start()
     for h in range(H):
         load(0, h).start()
         load(1, h).start()
@@ -145,6 +156,8 @@
         load(2, h).start()
         load(3, h).start()
 
+    for copy in small:
+        copy.wait()
     begin = s * T
     far = jnp.int32(1 << 24)
     total = jnp.int32(0)
@@ -179,9 +192,10 @@
 
     def share(way, b, o):
         to = peer(o)
+        heads = slice(*OUT_PARTS[way][b])
         return pltpu.make_async_remote_copy(
-            src_ref=share_out.at[way, b, place(g, to)],
-            dst_ref=share_in.at[way, b, m],
+            src_ref=share_out.at[way, place(g, to), heads],
+            dst_ref=share_in.at[way, m, heads],
             send_sem=share_ss.at[way, b, o],
             recv_sem=share_rs.at[way, b, o],
             device_id=member(to),
@@ -190,9 +204,10 @@
 
     def back(way, b, o):
         to = peer(o)
+        heads = slice(*BACK_PARTS[way][b])
         return pltpu.make_async_remote_copy(
-            src_ref=back_out.at[way, b, to],
-            dst_ref=back_in.at[way, b, mine],
+            src_ref=back_out.at[way, to, heads],
+            dst_ref=back_in.at[way, mine, heads],
             send_sem=back_ss.at[way, b, o],
             recv_sem=back_rs.at[way, b, o],
             device_id=member(to),
@@ -200,9 +215,10 @@
         )
 
     def tot(way, b, k):
+        heads = slice(*OUT_PARTS[way][b])
         return pltpu.make_async_remote_copy(
-            src_ref=tot_out.at[way, b],
-            dst_ref=tot_in.at[way, b, k - 1],
+            src_ref=tot_out.at[way, heads],
+            dst_ref=tot_in.at[way, k - 1, heads],
             send_sem=tot_ss.at[way, b, k - 1],
             recv_sem=tot_rs.at[way, b, k - 1],
             device_id=ally(k if way == 0 else G - k),
@@ -218,56 +234,61 @@
     def start_shares(way, b):
         for o in range(M - 1):
             share(way, b, o).start()
-        share_in[way, b, m] = share_out[way, b, mine]
+        for h in range(*OUT_PARTS[way][b]):
+            share_in[way, m, h] = share_out[way, mine, h]
 
     def start_totals(way, b):
         for o in reversed(range(M - 1)):
             share(way, b, o).wait_recv()
-        run = [jnp.zeros((ROWS, W), F32) for _ in range(HB)]
-        for i in range(M) if way == 0 else reversed(range(M)):
-            for e in range(HB):
-                h = b * HB + e
-                loc_s[b, i, e] = run[e]
-                run[e] = run[e] * one_s[i, h : h + 1] + share_in[way, b, i, e].astype(F32)
-        for e in range(HB):
-            tot_out[way, b, e] = run[e].astype(BF16)
+        for h in range(*OUT_PARTS[way][b]):
+            run = jnp.zeros((ROWS, W), F32)
+            for i in range(M) if way == 0 else reversed(range(M)):
+                loc_s[i, h] = run
+                run = run * one_s[i, h : h + 1] + share_in[way, i, h].astype(F32)
+            tot_out[way, h] = run.astype(BF16)
         for k in FAR_FIRST:
 
             @pl.when(sends(way, k))
             def _():
                 tot(way, b, k).start()
 
-    def start_back(way, b):
-        carry_s[b] = jnp.zeros((HB, ROWS, W), F32)
+    def gather_carry(way, b):
+        for h in range(*OUT_PARTS[way][b]):
+            carry_s[h] = jnp.zeros((ROWS, W), F32)
         for k in reversed(FAR_FIRST):
 
             @pl.when(receives(way, k))
             def _():
                 tot(way, b, k).wait_recv()
-                for e in range(HB):
-                    h = b * HB + e
-                    term = tot_in[way, b, k - 1, e].astype(F32)
+                for h in range(*OUT_PARTS[way][b]):
+                    term = tot_in[way, k - 1, h].astype(F32)
                     if k > 1:
                         term = term * coef_s[way, k - 2, h : h + 1]
-                    carry_s[b, e] = carry_s[b, e] + term
-
-        for e in range(HB):
-            h = b * HB + e
-            carry = carry_s[b, e]
-            for i in range(M):
-                back_out[way, b, i, e] = (
-                    loc_s[b, i, e] + carry * spread_s[way, i, h : h + 1]
-                ).astype(BF16)
-        for o in range(M - 1):
-            back(way, b, o).start()
-        back_in[way, b, mine] = back_out[way, b, m]
+                    carry_s[h] = carry_s[h] + term
+
+    def start_back(way):
+        ready = 0
+        for b, (lo, hi) in enumerate(BACK_PARTS[way]):
+            while ready < len(OUT_PARTS[way]) and OUT_PARTS[way][ready][0] < hi:
+                gather_carry(way, ready)
+                ready += 1
+            for h in range(lo, hi):
+                carry = carry_s[h]
+                for i in range(M):
+                    back_out[way, i, h] = (
+                        loc_s[i, h] + carry * spread_s[way, i, h : h + 1]
+                    ).astype(BF16)
+            for o in range(M - 1):
+                back(way, b, o).start()
+            for h in range(lo, hi):
+                back_in[way, mine, h] = back_out[way, m, h]
 
     def wait_back(way, b):
         for o in reversed(range(M - 1)):
             back(way, b, o).wait_recv()
 
-    def whole(way, b, e):
-        return back_in[way, b, :, e].reshape(W, W)
+    def whole(way, h):
+        return back_in[way, :, h].reshape(W, W)
 
     def forward(h, _):
         r = rates[h]
@@ -298,9 +319,8 @@
         dv_s[h, HALF:] = dot(w_s[h, HALF:, HALF:], d_s[h, HALF:], TN)
         return 0
 
-    for b in range(PARTS):
-        for e in range(HB):
-            h = b * HB + e
+    for b, (lo, hi) in enumerate(OUT_PARTS[0]):
+        for h in range(lo, hi):
             load(0, h).wait()
             load(1, h).wait()
             w_out = jnp.where(
@@ -310,7 +330,7 @@
             ks = (k_s[h].astype(F32) * w_out).astype(BF16)
             st = dot(ks, v_s[h], TN).astype(BF16)
             for i in range(M):
-                share_out[0, b, i, e] = st[i * ROWS : (i + 1) * ROWS]
+                share_out[0, i, h] = st[i * ROWS : (i + 1) * ROWS]
         if b == 0:
             pl.semaphore_wait(barrier, M - 1 + G - 1 + NHEAD - 1)
         start_shares(0, b)
@@ -345,19 +365,17 @@
         load(3, h).wait()
         g_s[h] = gain[:, h * W : (h + 1) * W] * og_s[h].astype(F32)
     lax.fori_loop(0, 3, forward, 0)
-    for b in range(PARTS):
+    for b in range(len(OUT_PARTS[0])):
         start_totals(0, b)
     lax.fori_loop(3, H, forward, 0)
-    for b in range(PARTS):
-        start_back(0, b)
+    start_back(0)
 
     squares_s[...] = jnp.zeros_like(squares_s)
     dots_s[...] = jnp.zeros_like(dots_s)
-    for b in range(PARTS):
+    for b, (lo, hi) in enumerate(BACK_PARTS[0]):
         wait_back(0, b)
-        for e in range(HB):
-            h = b * HB + e
-            inc = whole(0, b, e)
+        for h in range(lo, hi):
+            inc = whole(0, h)
             inc_s[h] = inc
             att = att_s[h] + wi_s[h] * dot(q_s[h], inc, NN)
             att_s[h] = att
@@ -399,13 +417,12 @@
     inv = jnp.broadcast_to(table[:, 0:1], (T, W))
     scale = jnp.broadcast_to(table[:, 1:2], (T, W))
 
-    for b in range(PARTS):
-        for e in range(HB):
-            h = b * HB + e
+    for b, (lo, hi) in enumerate(OUT_PARTS[1]):
+        for h in range(lo, hi):
             d_s[h] = (inv * g_s[h] - att_s[h] * scale).astype(BF16)
             gr = dot(qt_s[h], d_s[h], NN).astype(BF16)
             for i in range(M):
-                share_out[1, b, i, e] = gr[i * ROWS : (i + 1) * ROWS]
+                share_out[1, i, h] = gr[i * ROWS : (i + 1) * ROWS]
         start_shares(1, b)
 
     for h in range(H):
@@ -437,7 +454,7 @@
     gain_in[m] = gain_mine[...]
 
     lax.fori_loop(0, 3, backward, 0)
-    for b in range(PARTS):
+    for b in range(len(OUT_PARTS[1])):
         start_totals(1, b)
     for o in range(M - 1):
         gain_a(o).wait_recv()
@@ -449,8 +466,7 @@
         gain_b(k).start()
     gain_all[g] = part
     lax.fori_loop(3, H, backward, 0)
-    for b in range(PARTS):
-        start_back(1, b)
+    start_back(1)
     for k in range(1, G):
         gain_b(k).wait_recv()
     part = gain_all[0]
@@ -458,18 +474,19 @@
         part = part + gain_all[i]
     gg_ref[...] = part * (1.0 / math.sqrt(TOKENS))
 
-    for b in range(PARTS):
-        for o in range(M - 1):
-            share(0, b, o).wait_send()
-            back(0, b, o).wait_send()
-            share(1, b, o).wait_send()
-        for k in range(1, G):
-            for way in range(2):
+    for way in range(2):
+        for b in range(len(OUT_PARTS[way])):
+            for o in range(M - 1):
+                share(way, b, o).wait_send()
+            for k in range(1, G):
 
                 @pl.when(sends(way, k))
                 def _():
                     tot(way, b, k).wait_send()
 
+    for b in range(len(BACK_PARTS[0])):
+        for o in range(M - 1):
+            back(0, b, o).wait_send()
     for k in range(1, NHEAD):
         head_sum(k).wait_send()
     for o in range(M - 1):
@@ -477,14 +494,13 @@
     for k in range(1, G):
         gain_b(k).wait_send()
 
-    for b in range(PARTS):
+    for b, (lo, hi) in enumerate(BACK_PARTS[1]):
         wait_back(1, b)
-        for e in range(HB):
-            h = b * HB + e
-            out = whole(1, b, e)
+        for h in range(lo, hi):
+            out = whole(1, h)
             gk_s[:, h * W : (h + 1) * W] = (dk_s[h] + wo_s[h] * dot(v_s[h], out, NT)).astype(BF16)
             gv_s[:, h * W : (h + 1) * W] = (dv_s[h] + wo_s[h] * dot(k_s[h], out, NN)).astype(BF16)
-    for b in range(PARTS):
+    for b in range(len(BACK_PARTS[1])):
         for o in range(M - 1):
             back(1, b, o).wait_send()
 
@@ -513,7 +529,7 @@
     vmem = pl.BlockSpec(memory_space=pltpu.VMEM)
     dma = pltpu.SemaphoreType.DMA
     wide = (H, T, W)
-    shares = pltpu.VMEM((2, PARTS, M, HB, ROWS, W), BF16)
+    shares = pltpu.VMEM((2, M, H, ROWS, W), BF16)
     block = jax.ShapeDtypeStruct((T, H * W), BF16)
     row = jax.ShapeDtypeStruct((1, H * W), F32)
     gq, gk, gv, gg = pl.pallas_call(
@@ -524,7 +540,7 @@
             block,
             row,
         ),
-        in_specs=[smem, smem, vmem, hbm, hbm, hbm, hbm],
+        in_specs=[hbm] * 7,
         out_specs=(vmem,) * 4,
         scratch_shapes=[
             pltpu.VMEM(wide, BF16),
@@ -550,10 +566,10 @@
             pltpu.VMEM((2, M, 8, W), F32),
             shares,
             shares,
-            pltpu.VMEM((2, PARTS, HB, ROWS, W), BF16),
-            pltpu.VMEM((2, PARTS, G - 1, HB, ROWS, W), BF16),
-            pltpu.VMEM((PARTS, HB, ROWS, W), F32),
-            pltpu.VMEM((PARTS, M, HB, ROWS, W), F32),
+            pltpu.VMEM((2, H, ROWS, W), BF16),
+            pltpu.VMEM((2, G - 1, H, ROWS, W), BF16),
+            pltpu.VMEM((H, ROWS, W), F32),
+            pltpu.VMEM((M, H, ROWS, W), F32),
             shares,
             shares,
             pltpu.VMEM((2, T), F32),
@@ -562,6 +578,10 @@
             pltpu.VMEM((M, 1, H * W), F32),
             pltpu.VMEM((1, H * W), F32),
             pltpu.VMEM((G, 1, H * W), F32),
+            pltpu.SMEM((DOCS,), jnp.int32),
+            pltpu.SMEM((H,), F32),
+            pltpu.VMEM((1, H * W), F32),
+            dma((3,)),
             dma((4, H)),
             dma((2, PARTS, M - 1)),
             dma((2, PARTS, M - 1)),

time: 45.8 us -> 45.2 us (0.987)
  Pallas kernels: 44.4 us -> 43.8 us
    pallas_call x1, Pallas kernels: 42.3 us -> 41.7 us  [on_device(): pl.pallas_call(kernel, out_shape=(block, block, block, row), in_specs=[hb...]
where the time goes in v3:
time: 45.2 us; the launch traced here: 45.1 us
  Pallas kernels  43.8 us (97%)
  local copies, waits for them, and re-layouts  0.71 us (2%)
  between operations  0.66 us (1%)
    pallas_call x1, Pallas kernels, on_device(): pl.pallas_call(kernel, out_shape=(block, block, block, row), in_specs=[hb...  41.7 us
    pallas_call x1, Pallas kernels, on_device(): pl.pallas_call(write, out_shape=(block, block, block, jax.ShapeDtypeStruc...  2.07 us

profile of v3, /device:TPU:2, one launch (start us, length us, event | category | flops | bytes accessed | tf_op | source)
XLA Modules:
  0.0 45.1 jit_solution(13167204806952738602)
XLA Ops:
  0.6 0.0 copy-start.1
  0.6 0.0 copy-start
  0.7 0.7 %reshape.11.gain_hbm = f32[1,768]{1,0:T(1,128)S(1)} reshape(f32[768]{0:T(1024)} %param.12) | data formatting | bytes 6144 | tf_op jit(solution)/shard_map/reshape | solution.py:607
  1.4 0.0 copy-done.1
  1.4 0.0 copy-done
  1.4 41.7 %shard_map.102 = (bf16[512,768]{1,0:T(8,128)(2,1)S(1)}, bf16[512,768]{1,0:T(8,128)(2,1)S(1)}, bf16[512,768]{1,0:T(8,128)(2,1)S(1)}, f32[1,768]{1,0:T(1,128)S(1)}) custom-call(s32[32]{0:T(128)S(1)} %copy-done, f32[6]{0:T(128)S(1)} %copy-done.1, f32[1,768]{1,0:T(1,128)S(1)} %reshape.11.gain_hbm, bf16[512,768]{1,0:T(8,128)(2,1)} %q_hbm.1, ...), custom_call_target="tpu_custom_call" | custom-call | flops 2919235584 | bytes 3145728 | tf_op jit(solution)/shard_map/pallas_call | solution.py:535
  43.1 2.1 %shard_map.103 = (bf16[512,768]{1,0:T(8,128)(2,1)}, bf16[512,768]{1,0:T(8,128)(2,1)}, bf16[512,768]{1,0:T(8,128)(2,1)}, f32[768]{0:T(1024)}) custom-call(bf16[512,768]{1,0:T(8,128)(2,1)S(1)} %get-tuple-element.8.gq_s, bf16[512,768]{1,0:T(8,128)(2,1)S(1)} %get-tuple-element.9.gk_s, bf16[512,768]{1,0:T(8,128)(2,1)S(1)} %get-tuple-element.10.gv_s, ...), custom_call_target="tpu_custom_call" | custom-call | bytes 2359296 | tf_op jit(solution)/shard_map/pallas_call | solution.py:608
Async XLA Ops:
  0.6 0.7 %copy-start.1 = (f32[6]{0:T(128)S(1)}, f32[6]{0:T(128)}, u32[]{:S(2)}) copy-start(f32[6]{0:T(128)} %rates_hbm.1) | copy-start | bytes 76
  0.6 0.7 %copy-start = (s32[32]{0:T(128)S(1)}, s32[32]{0:T(128)}, u32[]{:S(2)}) copy-start(s32[32]{0:T(128)} %docs_hbm.1) | copy-start | bytes 388

commit v4 on v3

--- a/solution.py
+++ b/solution.py
@@ -126,14 +126,11 @@
         return (other * M + place(other, mine), hd)
 
     barrier = pltpu.get_barrier_semaphore()
-    for o in range(M - 1):
-        pl.semaphore_signal(barrier, inc=1, device_id=member(peer(o)), device_id_type=MESH)
-    for k in range(1, G):
-        pl.semaphore_signal(barrier, inc=1, device_id=ally(k), device_id_type=MESH)
-    for k in range(1, NHEAD):
-        pl.semaphore_signal(
-            barrier, inc=1, device_id=(s, lax.rem(hd + k, NHEAD)), device_id_type=MESH
-        )
+    reached = [member(peer(o)) for o in range(M - 1)]
+    reached = reached[:3] + [ally(k) for k in FAR_FIRST] + reached[3:]
+    reached += [(s, lax.rem(hd + k, NHEAD)) for k in (4, 5, 3, 2, 6, 1, 7)]
+    for device in reached:
+        pl.semaphore_signal(barrier, inc=1, device_id=device, device_id_type=MESH)
 
     hbm = (k_hbm, v_hbm, q_hbm, og_hbm)
     vmem = (k_s, v_s, q_s, og_s)
@@ -375,12 +372,19 @@
     for b, (lo, hi) in enumerate(BACK_PARTS[0]):
         wait_back(0, b)
         for h in range(lo, hi):
-            inc = whole(0, h)
-            inc_s[h] = inc
-            att = att_s[h] + wi_s[h] * dot(q_s[h], inc, NN)
-            att_s[h] = att
-            squares_s[...] += att * att
-            dots_s[...] += g_s[h] * att
+            inc_s[h] = whole(0, h)
+        for c in range(0, T, HALF):
+            rows = slice(c, c + HALF)
+            squares = squares_s[rows]
+            dots = dots_s[rows]
+            for h in range(lo, hi):
+                far_att = dot(q_s[h, rows], inc_s[h], NN)
+                att = att_s[h, rows] + wi_s[h, rows] * far_att
+                att_s[h, rows] = att
+                squares = squares + att * att
+                dots = dots + g_s[h, rows] * att
+            squares_s[rows] = squares
+            dots_s[rows] = dots
 
     def halves(x):
         high = x.astype(BF16)
@@ -508,19 +512,13 @@
 def write(gq_s, gk_s, gv_s, gg_s, gq_hbm, gk_hbm, gv_hbm, gg_ref, sem):
     held = (gq_s, gk_s, gv_s)
     outs = (gq_hbm, gk_hbm, gv_hbm)
-
-    def store(a, c):
-        rows = slice(c * W, (c + 1) * W)
-        return pltpu.make_async_copy(held[a].at[rows], outs[a].at[rows], sem.at[a, c])
-
-    for a in range(3):
-        for c in range(T // W):
-            store(a, c).start()
+    copies = [pltpu.make_async_copy(held[a], outs[a], sem.at[a]) for a in range(3)]
+    for copy in copies:
+        copy.start()
     for h in range(H):
         gg_ref[h * W : (h + 1) * W] = gg_s[0, h * W : (h + 1) * W]
-    for a in range(3):
-        for c in range(T // W):
-            store(a, c).wait()
+    for copy in copies:
+        copy.wait()
 
 
 def on_device(queries, keys, values, doc_lengths, decay_rates, gain, out_grad):
@@ -610,7 +608,7 @@
         out_shape=(block, block, block, jax.ShapeDtypeStruct((H * W,), F32)),
         in_specs=[vmem] * 4,
         out_specs=(hbm, hbm, hbm, vmem),
-        scratch_shapes=[dma((3, T // W))],
+        scratch_shapes=[dma((3,))],
         compiler_params=pltpu.CompilerParams(vmem_limit_bytes=51 << 20),
         cost_estimate=pl.CostEstimate(
             flops=0, bytes_accessed=3 * T * H * W * 2, transcendentals=0

time: 45.2 us -> 45.2 us (level)
  no operation moved by 1% of the time
where the time goes in v4:
time: 45.2 us; the launch traced here: 45 us
  Pallas kernels  43.7 us (97%)
  local copies, waits for them, and re-layouts  0.71 us (2%)
  between operations  0.66 us (1%)
    pallas_call x1, Pallas kernels, on_device(): pl.pallas_call(kernel, out_shape=(block, block, block, row), in_specs=[hb...  41.7 us
    pallas_call x1, Pallas kernels, on_device(): pl.pallas_call(write, out_shape=(block, block, block, jax.ShapeDtypeStruc...  2 us

profile of v4, /device:TPU:2, one launch (start us, length us, event | category | flops | bytes accessed | tf_op | source)
XLA Modules:
  0.0 45.0 jit_solution(11726831572514985232)
XLA Ops:
  0.6 0.0 copy-start.1
  0.6 0.0 copy-start
  0.7 0.7 %reshape.11.gain_hbm = f32[1,768]{1,0:T(1,128)S(1)} reshape(f32[768]{0:T(1024)} %param.12) | data formatting | bytes 6144 | tf_op jit(solution)/shard_map/reshape | solution.py:605
  1.4 0.0 copy-done.1
  1.4 0.0 copy-done
  1.4 41.7 %shard_map.102 = (bf16[512,768]{1,0:T(8,128)(2,1)S(1)}, bf16[512,768]{1,0:T(8,128)(2,1)S(1)}, bf16[512,768]{1,0:T(8,128)(2,1)S(1)}, f32[1,768]{1,0:T(1,128)S(1)}) custom-call(s32[32]{0:T(128)S(1)} %copy-done, f32[6]{0:T(128)S(1)} %copy-done.1, f32[1,768]{1,0:T(1,128)S(1)} %reshape.11.gain_hbm, bf16[512,768]{1,0:T(8,128)(2,1)} %q_hbm.1, ...), custom_call_target="tpu_custom_call" | custom-call | flops 2919235584 | bytes 3145728 | tf_op jit(solution)/shard_map/pallas_call | solution.py:533
  43.0 2.0 %shard_map.103 = (bf16[512,768]{1,0:T(8,128)(2,1)}, bf16[512,768]{1,0:T(8,128)(2,1)}, bf16[512,768]{1,0:T(8,128)(2,1)}, f32[768]{0:T(1024)}) custom-call(bf16[512,768]{1,0:T(8,128)(2,1)S(1)} %get-tuple-element.8.gq_s, bf16[512,768]{1,0:T(8,128)(2,1)S(1)} %get-tuple-element.9.gk_s, bf16[512,768]{1,0:T(8,128)(2,1)S(1)} %get-tuple-element.10.gv_s, ...), custom_call_target="tpu_custom_call" | custom-call | bytes 2359296 | tf_op jit(solution)/shard_map/pallas_call | solution.py:606
Async XLA Ops:
  0.6 0.7 %copy-start.1 = (f32[6]{0:T(128)S(1)}, f32[6]{0:T(128)}, u32[]{:S(2)}) copy-start(f32[6]{0:T(128)} %rates_hbm.1) | copy-start | bytes 76
  0.6 0.7 %copy-start = (s32[32]{0:T(128)S(1)}, s32[32]{0:T(128)}, u32[]{:S(2)}) copy-start(s32[32]{0:T(128)} %docs_hbm.1) | copy-start | bytes 388
